TPU v7x, 128 devices: a whole 4x4x4 slice. The times are simulated.
128 devices in a mesh: dp: 4 (over x), seq: 32 (over z, y, core).
Axes of the slice: x: 4, y: 4, z: 4, core: 2. Of those that a mesh axis runs over, the one named last changes fastest.
Arguments:
- ssm_input: bfloat16 [4, 8192, 3072], P('dp', 'seq'), may hold values from -6 to 6
- gate_input: bfloat16 [4, 8192, 3072], P('dp', 'seq'), may hold values from -6 to 6
- input_map: bfloat16 [4, 8192, 128], P('dp', 'seq'), may hold values from -0.52734375 to 0.52734375
- output_map: bfloat16 [4, 8192, 128], P('dp', 'seq'), may hold values from -6 to 6
- step_logit: bfloat16 [4, 8192, 48], P('dp', 'seq'), may hold values from -5 to 5
- step_bias: float32 [48], replicated, may hold values from -1 to 1
- decay_rate: float32 [48], replicated, may hold values from 6.1035156e-07 to 0.05
- skip_gain: float32 [48], replicated, may hold values from 0.5 to 1.5
- norm_gain: float32 [3072], replicated, may hold values from 0.1 to 1.9
- out_weight: bfloat16 [3072, 1536], replicated, may hold values from -0.109375 to 0.109375
- resets: int32 [4, 4], P('dp'), may hold values from 1 to 8191
- out_grad: bfloat16 [4, 8192, 1536], P('dp', 'seq'), may hold values from -6 to 6
Outputs:
- mixed_out: bfloat16 [4, 8192, 1536], P('dp', 'seq')
- grad_input: bfloat16 [4, 8192, 3072], P('dp', 'seq')
- grad_gate: bfloat16 [4, 8192, 3072], P('dp', 'seq')
- grad_inmap: bfloat16 [4, 8192, 128], P('dp', 'seq')
- grad_outmap: bfloat16 [4, 8192, 128], P('dp', 'seq')
- grad_step: bfloat16 [4, 8192, 48], P('dp', 'seq')
- grad_bias: float32 [48], replicated
- grad_rate: float32 [48], replicated
- grad_skip: float32 [48], replicated
- grad_gain: float32 [3072], replicated
- grad_weight: float32 [3072, 1536], P('seq')
All inputs are finite; a program needn't handle non-finite values.
Results may differ from a plain program's by a relative error of at most 0.0049.
Values sent between devices are 32-bit elements; how exact they have to be, the bound alone decides.
A program may use at most 384 MiB of HBM per device.

v0:
```python
import jax
import jax.numpy as jnp
from jax import lax
from jax.sharding import PartitionSpec as P

SPAN = 128
highest = lax.Precision.HIGHEST


def prefix(shard, axis, combine, identity, reverse):
    count, place = (lax.axis_size(axis), lax.axis_index(axis))
    everything = jax.tree.map(lambda part: lax.all_gather(part, axis), shard)
    start = jax.tree.map(
        lambda part, zero: jnp.broadcast_to(jnp.asarray(zero, part.dtype), part.shape),
        shard,
        identity,
    )

    def hop(k, before):
        at = count - 1 - k if reverse else k
        reached = at > place if reverse else at < place
        new = combine(before, jax.tree.map(lambda part: part[at], everything))
        return jax.tree.map(lambda a, b: jnp.where(reached, a, b), new, before)

    return lax.fori_loop(0, count, hop, start)


def block_step(state_in, inputs):
    x_blk, b_blk, c_blk, step_blk, decay_blk, flag_blk = inputs
    cumulative = jnp.cumsum(decay_blk, axis=0)
    counts = jnp.cumsum(flag_blk)
    block_len = flag_blk.shape[0]
    row_ids = lax.broadcasted_iota(jnp.int32, (block_len, block_len), 0)
    col_ids = lax.broadcasted_iota(jnp.int32, (block_len, block_len), 1)
    in_mask = ((row_ids >= col_ids) & (counts[:, None] == counts[None, :]))[:, :, None]
    gap_vals = cumulative[:, None, :] - cumulative[None, :, :]
    decay_mat = jnp.where(in_mask, jnp.exp(jnp.where(in_mask, gap_vals, 0.0)), 0.0)
    gram_mat = jnp.einsum("in,jn->ij", c_blk, b_blk, precision=highest)
    mixing = gram_mat[:, :, None] * decay_mat * step_blk[None, :, :]
    y_blk = jnp.einsum("ijh,jhp->ihp", mixing, x_blk, precision=highest)
    opened = (counts == 0)[:, None]
    from_start = jnp.where(opened, jnp.exp(jnp.where(opened, cumulative, 0.0)), 0.0)
    y_blk = y_blk + from_start[:, :, None] * jnp.einsum(
        "in,hpn->ihp", c_blk, state_in, precision=highest
    )
    keep_mask = (counts == counts[-1])[:, None]
    tail_weights = (
        jnp.where(
            keep_mask, jnp.exp(jnp.where(keep_mask, cumulative[-1][None, :] - cumulative, 0.0)), 0.0
        )
        * step_blk
    )
    whole_decay = jnp.where(counts[-1] == 0, jnp.exp(cumulative[-1]), 0.0)
    new_state = whole_decay[:, None, None] * state_in + jnp.einsum(
        "jhp,jn->hpn", tail_weights[:, :, None] * x_blk, b_blk, precision=highest
    )
    return (new_state, y_blk)


def ssd_blocks(x_heads, b_float, c_float, step_vals, log_decay, flags, state_in):
    num_blocks = x_heads.shape[0] // SPAN

    def to_blocks(values):
        return values.reshape((num_blocks, SPAN) + values.shape[1:])

    final_state, y_blocks = lax.scan(
        block_step,
        state_in,
        (
            to_blocks(x_heads),
            to_blocks(b_float),
            to_blocks(c_float),
            to_blocks(step_vals),
            to_blocks(log_decay),
            to_blocks(flags),
        ),
    )
    return (final_state, y_blocks.reshape(x_heads.shape))


def gate_norm(y_ssd, x_float, z_float, skip_gain, norm_gain):
    num_heads = skip_gain.shape[0]
    rows_here = x_float.shape[0]
    y_full = y_ssd.reshape(rows_here, -1) + (
        x_float.reshape(rows_here, num_heads, -1) * skip_gain[None, :, None]
    ).reshape(x_float.shape)
    gated_vals = y_full * jax.nn.silu(z_float)
    scale_inv = lax.rsqrt(jnp.mean(gated_vals * gated_vals, axis=-1, keepdims=True) + 1e-05)
    return gated_vals * scale_inv * norm_gain


def step_sizes(logit_vals, bias_in, rate_in):
    step_vals = jax.nn.softplus(logit_vals + bias_in)
    return (step_vals, -rate_in * step_vals)


def combine(earlier, later):
    return (earlier[0] * later[0], later[0][:, None, None] * earlier[1] + later[1])


def per_device(
    ssm_input,
    gate_input,
    input_map,
    output_map,
    step_logit,
    step_bias,
    decay_rate,
    skip_gain,
    norm_gain,
    out_weight,
    resets,
    out_grad,
):
    rows_here = ssm_input.shape[1]
    num_heads = step_bias.shape[0]
    x_float = ssm_input[0].astype(jnp.float32)
    z_float = gate_input[0].astype(jnp.float32)
    b_float = input_map[0].astype(jnp.float32)
    c_float = output_map[0].astype(jnp.float32)
    logit_float = step_logit[0].astype(jnp.float32)
    inner_width = x_float.shape[1]
    head_size = inner_width // num_heads
    x_heads = x_float.reshape(rows_here, num_heads, head_size)
    positions = lax.axis_index("seq") * rows_here + lax.iota(jnp.int32, rows_here)
    flags = jnp.max((positions[:, None] == resets[0][None, :]).astype(jnp.int32), axis=1)
    counts = jnp.cumsum(flags)
    opened = (counts == 0)[:, None]
    clean_shard = counts[-1] == 0
    empty_state = jnp.zeros((num_heads, head_size, b_float.shape[1]), jnp.float32)
    identity = (jnp.ones((num_heads,), jnp.float32), empty_state)
    step_vals, log_decay = step_sizes(logit_float, step_bias, decay_rate)
    cumulative = jnp.cumsum(log_decay, axis=0)
    from_start = jnp.where(opened, jnp.exp(jnp.where(opened, cumulative, 0.0)), 0.0)
    shard_through = jnp.where(clean_shard, jnp.exp(cumulative[-1]), 0.0)
    step_vals, cumulative, from_start, through = (step_vals, cumulative, from_start, shard_through)
    keep_mask = (counts == counts[-1])[:, None]
    tail_weights = (
        jnp.where(
            keep_mask, jnp.exp(jnp.where(keep_mask, cumulative[-1][None, :] - cumulative, 0.0)), 0.0
        )
        * step_vals
    )
    shard_state = jnp.einsum(
        "thp,tn->hpn", tail_weights[:, :, None] * x_heads, b_float, precision=highest
    )
    incoming = prefix((through, shard_state), "seq", combine, identity, False)[1]

    def from_incoming(x_part, b_part, c_part, logit_vals, bias_in, rate_in):
        step_part, decay_part = step_sizes(logit_vals, bias_in, rate_in)
        return ssd_blocks(x_part, b_part, c_part, step_part, decay_part, flags, incoming)

    (final_state, y_ssd), ssd_pullback = jax.vjp(
        from_incoming, x_heads, b_float, c_float, logit_float, step_bias, decay_rate
    )
    normed_f, post_pullback = jax.vjp(gate_norm, y_ssd, x_float, z_float, skip_gain, norm_gain)
    normed = normed_f.astype(jnp.bfloat16)
    mixed = jnp.dot(normed, out_weight, preferred_element_type=jnp.float32).astype(jnp.bfloat16)
    grad_rows = out_grad[0]
    normed_grad = lax.dot_general(
        grad_rows, out_weight, (((1,), (1,)), ((), ())), preferred_element_type=jnp.float32
    )
    y_grad, x_grad_skip, z_grad, skip_grad, gain_grad = post_pullback(normed_grad)
    start_grad = jnp.einsum(
        "thp,tn->hpn", from_start[:, :, None] * y_grad, c_float, precision=highest
    )
    later_grad = prefix((through, start_grad), "seq", combine, identity, True)[1]
    x_grad, b_grad, c_grad, logit_grad, bias_grad, rate_grad = ssd_pullback((later_grad, y_grad))
    bias_sum, rate_sum, skip_sum, gain_sum = lax.psum(
        (bias_grad, rate_grad, skip_grad, gain_grad), ("dp", "seq")
    )
    seq_rows = lax.psum_scatter(
        lax.dot_general(
            normed, grad_rows, (((0,), (0,)), ((), ())), preferred_element_type=jnp.float32
        ),
        "seq",
        scatter_dimension=0,
        tiled=True,
    )
    weight_grad = lax.psum(seq_rows, "dp")
    grad_input = (x_grad.reshape(rows_here, inner_width) + x_grad_skip).astype(jnp.bfloat16)
    return (
        mixed[None],
        grad_input[None],
        z_grad.astype(jnp.bfloat16)[None],
        b_grad.astype(jnp.bfloat16)[None],
        c_grad.astype(jnp.bfloat16)[None],
        logit_grad.astype(jnp.bfloat16)[None],
        bias_sum,
        rate_sum,
        skip_sum,
        gain_sum,
        weight_grad,
    )


def solution(mesh):
    placed = (
        P("dp", "seq", None),
        P("dp", "seq", None),
        P("dp", "seq", None),
        P("dp", "seq", None),
        P("dp", "seq", None),
        P(),
        P(),
        P(),
        P(),
        P(),
        P("dp", None),
        P("dp", "seq", None),
    )
    return jax.shard_map(
        per_device,
        mesh=mesh,
        in_specs=placed,
        out_specs=(
            P("dp", "seq", None),
            P("dp", "seq", None),
            P("dp", "seq", None),
            P("dp", "seq", None),
            P("dp", "seq", None),
            P("dp", "seq", None),
            P(),
            P(),
            P(),
            P(),
            P("seq", None),
        ),
        check_vma=False,
    )
```

profile of v0, /device:TPU:1, one launch (start us, length us, event | category | flops | bytes accessed | tf_op | source)
XLA Modules:
  0.0 973.6 jit_solution(15452090480564412764)
XLA Ops:
  17.8 3.7 copy.144
  21.5 4.1 convert_multiply_fusion
  25.6 3.6 copy.145
  29.2 4.5 fusion.162
  34.0 3.1 copy.147
  37.1 5.3 reshape.1003
  42.5 4.0 copy.148
  46.5 3.2 copy.152
  49.7 5.5 reshape.1008
  55.9 24.0 %all-gather.2 = f32[32,1,48]{2,1,0:T(1,128)S(1)} all-gather(f32[1,1,48]{2,1,0:T(1,128)S(1)} %bitcast.581), channel_id=1, replica_groups=mesh['dp'=4,'seq'=32] {'seq'}, dimensions={0}, use_global_device_ids=true | all-gather | bytes 6336 | tf_op jit(solution)/shard_map/all_gather | solution.py:12
  79.9 115.2 %all-gather.6.cloned.1.call-done = f32[1536,64,128]{2,1,0:T(8,128)} async-done(((f32[48,64,128]{2,1,0:T(8,128)}), f32[1536,64,128]{2,1,0:T(8,128)}) %all-gather.6.cloned.1.call-update) | async-done | bytes 50331664 | tf_op jit(solution)/shard_map/all_gather | solution.py:12
  195.1 58.0 %while.116 = (s32[]{:T(128)}, f32[48,64,128]{2,1,0:T(8,128)S(1)}, s32[]{:T(128)}, f32[32,48]{1,0:T(8,128)S(1)}, f32[32,48,64,128]{3,2,1,0:T(8,128)}, /*index=5*/s32[]{:T(128)}, s32[]{:T(128)}) while((s32[]{:T(128)}, f32[48,64,128]{2,1,0:T(8,128)S(1)}, s32[]{:T(128)}, f32[32,48]{1,0:T(8,128)S(1)}, f32[32,48,64,128]{3,2,1,0:T(8,128)}, ...), condition=%wide.region_6.7_spmd.clone, body=%wide.region_5.6_spmd.clone.sunk | while | flops 1572868 | bytes 4719273 | solution.py:25
  259.2 154.5 %while.115 = (s32[]{:T(128)}, f32[48,64,128]{2,1,0:T(8,128)S(1)}, f32[2,128,48,64]{1,3,2,0:T(8,128)}, pred[2,128,128,48]{2,1,3,0:T(32,128)(4,1)}, f32[2,128,128,...) while((s32[]{:T(128)}, f32[48,64,128]{2,1,0:T(8,128)S(1)}, ...), condition=%wide.region_10.11_spmd.clone, body=%wide.region_7.10_spmd.clone.sunk | while | flops 1848273152 | bytes 111490832 | solution.py:66
  262.9 11.3 %broadcast_multiply_fusion.4 = (f32[1,128,128,48]{3,2,1,0:T(8,128)}, f32[1,128,128,48]{3,2,1,0:T(8,128)}, f32[1,128,128,48]{3,2,1,0:T(8,128)}, f32[1,128,128,48]{3,2,1,0:T(8,128)}) fusion(f32[128,48]{1,0:T(8,128)S(1)} %get-tuple-element.2450, f32[128,48]{1,0:T(8,128)S(1)} %reduce_window_sum.92, pred[128,128]{1,0:T(8,128)(4,1)S(1)} %fusion.251, ...), kind=kLoop, calls=%fused_computation.99.clone.1 | loop fusion | flops 3932160 | bytes 12713984 | tf_op jit(solution)/shard_map/jvp()/while/body/eval_jaxpr/mul | solution.py:39
  274.2 6.9 copy.272
  281.1 6.8 copy.273
  287.9 6.3 constant_dynamic-update-slice_fusion.23
  294.2 6.9 copy.269
  301.1 6.8 copy.270
  307.9 6.4 constant_dynamic-update-slice_fusion.21
  314.5 2.6 bitcast_dynamic-update-slice_fusion.11
  317.1 7.6 bitcast_dynamic-update-slice_fusion.13
  324.7 2.9 multiply_dynamic-update-slice_fusion.2
  339.9 11.3 %broadcast_multiply_fusion.4 = (f32[1,128,128,48]{3,2,1,0:T(8,128)}, f32[1,128,128,48]{3,2,1,0:T(8,128)}, f32[1,128,128,48]{3,2,1,0:T(8,128)}, f32[1,128,128,48]{3,2,1,0:T(8,128)}) fusion(f32[128,48]{1,0:T(8,128)S(1)} %get-tuple-element.2450, f32[128,48]{1,0:T(8,128)S(1)} %reduce_window_sum.92, pred[128,128]{1,0:T(8,128)(4,1)S(1)} %fusion.251, ...), kind=kLoop, calls=%fused_computation.99.clone.1 | loop fusion | flops 3932160 | bytes 12713984 | tf_op jit(solution)/shard_map/jvp()/while/body/eval_jaxpr/mul | solution.py:39
  351.2 6.9 copy.272
  358.1 6.8 copy.273
  365.0 6.3 constant_dynamic-update-slice_fusion.23
  371.2 6.9 copy.269
  378.1 6.8 copy.270
  384.9 6.4 constant_dynamic-update-slice_fusion.21
  391.6 2.6 bitcast_dynamic-update-slice_fusion.11
  394.2 7.6 bitcast_dynamic-update-slice_fusion.13
  401.8 2.9 multiply_dynamic-update-slice_fusion.2
  413.7 7.7 multiply_reduce_fusion.2
  421.4 3.9 multiply_convert_fusion
  425.3 7.8 fusion.146
  436.0 3.6 copy.153
  439.6 6.5 copy.180
  446.1 6.4 reshape.1022
  452.5 10.8 %multiply_reduce_fusion = (f32[3072]{0:T(1024)}, f32[256]{0:T(256)S(1)}, f32[256,3072]{1,0:T(8,128)S(1)}) fusion(f32[256]{0:T(256)S(1)} %bitcast_rsqrt_fusion, bf16[1,256,3072]{2,1,0:T(8,128)(2,1)} %param.21, f32[256,3072]{1,0:T(8,128)} %reshape.1022, f32[3072]{0:T(1024)S(1)} %mul.708, bf16[1,256,3072]{2,1,0:T(8,128)(2,1)S(1)} %copy-done.8, ...), kind=kOutput, calls=%fused_computation.207 | convolution fusion | flops 2427712256 | bytes 19699712 | tf_op jit(solution)/shard_map/dot_general | solution.py:160
  463.3 3.9 fusion.142
  471.0 4.1 copy.154
  475.1 4.6 fusion.160
  480.5 6.1 reshape.1023
  486.6 7.1 copy.158
  494.4 10.0 %fusion.143 = bf16[1,256,1536]{2,1,0:T(8,128)(2,1)} fusion(bf16[3072,1536]{1,0:T(8,128)(2,1)} %param.29, f32[3072]{0:T(1024)S(1)} %copy-done.27, f32[256]{0:T(256)S(1)} %bitcast_rsqrt_fusion, f32[256,3072]{1,0:T(8,128)} %reshape.1022, bf16[1,256,3072]{2,1,0:T(8,128)(2,1)} %param.20, f32[3072]{0:T(1024)S(1)} %mul.708, bf16[1,256,3072]{2,1,0:T(8,128)(2,1)} %param.21), kind=kOutput, calls=%fused_computation.213 | convolution fusion | flops 2425749504 | bytes 16540672 | tf_op jit(solution)/shard_map/dot_general | solution.py:158
  504.3 48.3 %reduce-scatter.2.cloned.1.call-done = f32[96,1536]{1,0:T(8,128)} async-done(((f32[3072,1536]{1,0:T(8,128)}), f32[96,1536]{1,0:T(8,128)}) %reduce-scatter.2.cloned.1.call-update) | async-done | bytes 589840 | tf_op jit(solution)/shard_map/reduce_scatter | solution.py:172
  552.7 161.2 %all-gather.8.cloned.1.call-done = f32[1536,64,128]{2,1,0:T(8,128)} async-done(((f32[48,64,128]{2,1,0:T(8,128)}), f32[1536,64,128]{2,1,0:T(8,128)}) %all-gather.8.cloned.1.call-update) | async-done | bytes 50331664 | tf_op jit(solution)/shard_map/all_gather | solution.py:12
  713.8 79.9 %while.117 = (s32[]{:T(128)}, f32[48,64,128]{2,1,0:T(8,128)S(1)}, s32[]{:T(128)}, f32[32,48]{1,0:T(8,128)}, f32[32,48,64,128]{3,2,1,0:T(8,128)}, /*index=5*/s32[]{:T(128)}, s32[]{:T(128)}, s32[]{:T(128)}, s32[]{:T(128)}) while((s32[]{:T(128)}, f32[48,64,128]{2,1,0:T(8,128)S(1)}, s32[]{:T(128)}, f32[32,48]{1,0:T(8,128)}, ...), condition=%wide.region_14.15_spmd.clone, body=%wide.region_13.14_spmd.clone.sunk | while | flops 1572872 | bytes 4719335 | solution.py:25
  797.9 83.0 %while.114 = (s32[]{:T(128)}, f32[48,64,128]{2,1,0:T(8,128)S(1)}, f32[2,128,48,64]{1,3,2,0:T(8,128)}, bf16[2,128,128]{2,1,0:T(8,128)(2,1)}, bf16[2,128,128]{2,1,...) while((s32[]{:T(128)}, f32[48,64,128]{2,1,0:T(8,128)S(1)}, ...), condition=%wide.region_25.26_spmd, body=%wide.region_15.25_spmd.sunk | while | flops 3688450048 | bytes 77251128 | solution.py:66
  798.9 11.1 %fusion.235 = (f32[128,48]{0,1:T(8,128)S(1)}, f32[128,48]{0,1:T(8,128)S(1)}, f32[128,128]{1,0:T(8,128)S(1)}, f32[128,48]{0,1:T(8,128)S(1)}) fusion(f32[2,128,128,48]{2,1,3,0:T(8,128)} %get-tuple-element.2728, s32[]{:T(128)S(6)} %sub.274, f32[128,48]{0,1:T(8,128)S(1)} %dynamic-slice_bitcast_fusion.18, ...), kind=kOutput, calls=%fused_computation.91.clone.1 | convolution fusion | flops 612595712 | bytes 13600256 | tf_op jit(solution)/shard_map/transpose(jvp())/while/body/eval_jaxpr/ijh,jhp->ihp/dot_general | solution.py:40
  812.0 4.0 fusion.233
  821.9 4.7 fusion.237
  827.4 4.0 fusion.234
  831.8 5.5 bitcast_dynamic-update-slice_fusion.10
  840.2 11.1 %fusion.235 = (f32[128,48]{0,1:T(8,128)S(1)}, f32[128,48]{0,1:T(8,128)S(1)}, f32[128,128]{1,0:T(8,128)S(1)}, f32[128,48]{0,1:T(8,128)S(1)}) fusion(f32[2,128,128,48]{2,1,3,0:T(8,128)} %get-tuple-element.2728, s32[]{:T(128)S(6)} %sub.274, f32[128,48]{0,1:T(8,128)S(1)} %dynamic-slice_bitcast_fusion.18, ...), kind=kOutput, calls=%fused_computation.91.clone.1 | convolution fusion | flops 612595712 | bytes 13600256 | tf_op jit(solution)/shard_map/transpose(jvp())/while/body/eval_jaxpr/ijh,jhp->ihp/dot_general | solution.py:40
  853.3 4.0 fusion.233
  863.2 4.7 fusion.237
  868.8 4.0 fusion.234
  873.2 5.4 bitcast_dynamic-update-slice_fusion.10
  883.0 6.1 copy.183
  889.1 5.8 reshape.1024
  895.7 64.7 %all-reduce.2 = (f32[48]{0:T(128)}, f32[48]{0:T(128)}, f32[48]{0:T(128)}, f32[3072]{0:T(1024)}) all-reduce(f32[48]{0:T(128)S(1)} %get-tuple-element.1778, f32[48]{0:T(128)S(1)} %neg.49, f32[48]{0:T(128)S(1)} %copy-done.36, f32[3072]{0:T(1024)S(1)} %copy-done.32), channel_id=1, replica_groups=mesh['dp'=4,'seq'=32] {'dp','seq'}, use_global_device_ids=true, to_apply=%region_27.28 | all-reduce | flops 3216 | bytes 25728 | tf_op jit(solution)/shard_map/psum | solution.py:169
  960.4 4.6 fusion.145
  (449 shorter events, 217.1 us)
Async XLA Ops:
  7.2 418.2 %copy-start = (bf16[1,256,1536]{2,1,0:T(8,128)(2,1)S(1)}, bf16[1,256,1536]{2,1,0:T(8,128)(2,1)}, u32[]{:S(2)}) copy-start(bf16[1,256,1536]{2,1,0:T(8,128)(2,1)} %param.31) | copy-start | bytes 2359300
  7.2 187.9 %all-gather.6.cloned.1.call-start = ((), (), s32[]{:S(2)}) async-start(), calls=%async_computation.3 | async-start | bytes 51904512 | tf_op jit(solution)/shard_map/all_gather | solution.py:12
  12.5 67.4 %copy-start.33 = (f32[48]{0:T(128)}, f32[48]{0:T(128)S(1)}, u32[]{:S(2)}) copy-start(f32[48]{0:T(128)S(1)} %neg.43) | copy-start | bytes 580
  17.8 3.7 copy-start.7
  25.6 3.6 copy-start.16
  29.2 4.6 copy-start.14
  33.8 518.9 %reduce-scatter.2.cloned.1.call-start = ((), (), s32[]{:S(2)}) async-start(), calls=%async_computation.1 | async-start | bytes 19464192 | tf_op jit(solution)/shard_map/reduce_scatter | solution.py:172
  33.9 45.9 %copy-start.12 = (f32[1,256,48]{2,1,0:T(8,128)}, f32[1,256,48]{2,1,0:T(8,128)S(1)}, u32[]{:S(2)}) copy-start(f32[1,256,48]{2,1,0:T(8,128)S(1)} %copy.179) | copy-start | bytes 147460
  42.5 4.0 copy-start.17
  49.7 5.5 copy-start.26
  49.7 30.2 %copy-start.29 = (f32[48]{0:T(128)S(1)}, f32[48]{0:T(128)}, u32[]{:S(2)}) copy-start(f32[48]{0:T(128)} %param.25) | copy-start | bytes 580
  253.1 4.1 copy-start.28
  314.5 2.6 copy-start.2
  328.3 2.5 copy-start.3
  330.7 3.5 copy-start.21
  330.7 3.5 copy-start.40
  330.7 3.6 copy-start.31
  330.7 3.6 copy-start.37
  330.8 4.9 copy-start.43
  334.3 2.2 copy-start.22
  334.3 2.1 copy-start.41
  334.4 2.1 copy-start.38
  335.7 0.7 copy-start.44
  391.6 2.6 copy-start.2
  405.3 2.5 copy-start.3
  407.8 3.5 copy-start.21
  407.8 3.5 copy-start.40
  407.8 3.5 copy-start.31
  407.8 3.6 copy-start.37
  407.8 4.9 copy-start.43
  411.3 2.2 copy-start.22
  411.3 2.1 copy-start.41
  411.4 2.1 copy-start.38
  413.7 7.7 copy-start.20
  433.1 0.8 copy-start.19
  433.2 280.7 %all-gather.8.cloned.1.call-start = ((), (), s32[]{:S(2)}) async-start(), calls=%async_computation.4 | async-start | bytes 51904512 | tf_op jit(solution)/shard_map/all_gather | solution.py:12
  446.1 6.4 copy-start.8
  446.1 6.4 copy-start.27
  452.5 10.8 %copy-start.10 = (f32[256,3072]{1,0:T(8,128)S(1)}, f32[256,3072]{1,0:T(8,128)}, u32[]{:S(2)}) copy-start(f32[256,3072]{1,0:T(8,128)} %reshape.1022) | copy-start | bytes 9437188
  452.5 10.8 %copy-start.11 = (bf16[1,256,3072]{2,1,0:T(8,128)(2,1)S(1)}, bf16[1,256,3072]{2,1,0:T(8,128)(2,1)}, u32[]{:S(2)}) copy-start(bf16[1,256,3072]{2,1,0:T(8,128)(2,1)} %param.21) | copy-start | bytes 4718596
  463.3 5.6 copy-start.9
  467.2 1.6 copy-start.6
  471.0 4.1 copy-start.18
  479.8 485.2 %all-reduce.5.cloned.1.call-start = ((), (), s32[]{:S(2)}) async-start(), calls=%async_computation.2 | async-start | bytes 1179648 | tf_op jit(solution)/shard_map/psum | solution.py:180
  793.7 4.2 copy-start.23
  793.7 4.1 copy-start.39
  793.7 4.1 copy-start.42
  793.7 4.1 copy-start.45
  797.9 84.8 %copy-start.13 = (f32[1,256,48]{2,1,0:T(8,128)S(1)}, f32[1,256,48]{2,1,0:T(8,128)}, u32[]{:S(2)}) copy-start(f32[1,256,48]{2,1,0:T(8,128)} %copy-done.12) | copy-start | bytes 147460
  797.9 84.8 %copy-start.30 = (f32[48]{0:T(128)S(1)}, f32[48]{0:T(128)}, u32[]{:S(2)}) copy-start(f32[48]{0:T(128)} %param.25) | copy-start | bytes 580
  797.9 84.8 %copy-start.34 = (f32[48]{0:T(128)S(1)}, f32[48]{0:T(128)}, u32[]{:S(2)}) copy-start(f32[48]{0:T(128)} %copy-done.33) | copy-start | bytes 580
  798.9 11.2 %copy-start.5 = (f32[2,48,64,128]{3,2,1,0:T(8,128)S(1)}, f32[2,48,64,128]{3,2,1,0:T(8,128)}, u32[]{:S(2)}) copy-start(f32[2,48,64,128]{3,2,1,0:T(8,128)} %get-tuple-element.2715) | copy-start | bytes 9437188 | tf_op jit(solution)/shard_map/transpose(jvp())/while
  821.9 9.6 copy-start.24
  821.9 9.9 %copy-start.1 = (f32[2,128,48,64]{1,3,2,0:T(8,128)S(1)}, f32[2,128,48,64]{1,3,2,0:T(8,128)}, u32[]{:S(2)}) copy-start(f32[2,128,48,64]{1,3,2,0:T(8,128)} %get-tuple-element.2706) | copy-start | bytes 9437188 | tf_op jit(solution)/shard_map/transpose(jvp())/while
  821.9 9.9 %copy-start.4 = (f32[128,48,64]{0,2,1:T(8,128)S(1)}, f32[128,48,64]{0,2,1:T(8,128)}, u32[]{:S(2)}) copy-start(f32[128,48,64]{0,2,1:T(8,128)} %get-tuple-element.2407) | copy-start | bytes 4718596 | tf_op jit(solution)/shard_map/transpose(jvp())/while
  831.8 5.5 copy-start.25
  840.2 11.2 %copy-start.5 = (f32[2,48,64,128]{3,2,1,0:T(8,128)S(1)}, f32[2,48,64,128]{3,2,1,0:T(8,128)}, u32[]{:S(2)}) copy-start(f32[2,48,64,128]{3,2,1,0:T(8,128)} %get-tuple-element.2715) | copy-start | bytes 9437188 | tf_op jit(solution)/shard_map/transpose(jvp())/while
  863.2 9.6 copy-start.24
  863.2 9.9 %copy-start.1 = (f32[2,128,48,64]{1,3,2,0:T(8,128)S(1)}, f32[2,128,48,64]{1,3,2,0:T(8,128)}, u32[]{:S(2)}) copy-start(f32[2,128,48,64]{1,3,2,0:T(8,128)} %get-tuple-element.2706) | copy-start | bytes 9437188 | tf_op jit(solution)/shard_map/transpose(jvp())/while
  863.2 9.9 %copy-start.4 = (f32[128,48,64]{0,2,1:T(8,128)S(1)}, f32[128,48,64]{0,2,1:T(8,128)}, u32[]{:S(2)}) copy-start(f32[128,48,64]{0,2,1:T(8,128)} %get-tuple-element.2407) | copy-start | bytes 4718596 | tf_op jit(solution)/shard_map/transpose(jvp())/while
  873.1 5.4 copy-start.25
  889.1 5.9 copy-start.15
  889.1 6.6 copy-start.32
  889.1 6.6 copy-start.36
  (2 other events, 1.4 us)
Sparse Core Ops, SparseCore 0:
  33.9 161.1 all-gather.5
  433.3 119.3 reduce-scatter.1
  555.8 158.0 all-gather.7
  716.2 40.1 all-reduce.4
where the time goes:
time: 984 us; the launch traced here: 974 us
  waiting for transfers between devices  325 us (33%)
  local copies, waits for them, and re-layouts  220 us (22%)
  other arithmetic  192 us (20%)
  matrix products  128 us (13%)
  blocking collectives  88.7 us (9%)
  between operations  15.1 us (2%)
    all_gather x2, waiting for transfers between devices, prefix(): everything = jax.tree.map(lambda part: lax.all_gather(part, axis), shard)  276 us
    select_n x64, other arithmetic, hop(): return jax.tree.map(lambda a, b: jnp.where(reached, a, b), new, before)  113 us
    dynamic_update_slice x44, local copies, waits for them, and re-layouts, ssd_blocks(): lax.scan(block_step, state_in, (to_blocks(x_heads), to_blocks(b_float), t...  89 us
    psum x1, blocking collectives, per_device(): lax.psum((bias_grad, rate_grad, skip_grad, gain_grad), ('dp', 'seq'))  64.7 us
    reduce_scatter x1, waiting for transfers between devices, per_device(): lax.psum_scatter(lax.dot_general(normed, grad_rows, (((0,), (0,)), ((), (...  48.3 us
    dot_general x6, matrix products, block_step(): y_blk = jnp.einsum('ijh,jhp->ihp', mixing, x_blk, precision=highest)  48.3 us
    all_gather x1, blocking collectives, prefix(): everything = jax.tree.map(lambda part: lax.all_gather(part, axis), shard)  24 us
    mul x2, other arithmetic, block_step(): mixing = gram_mat[:, :, None] * decay_mat * step_blk[None, :, :]  22.6 us
  transfers between devices with their start and end apart: 4, of which 3 were waited for; matrix products, arithmetic and copies ran while one was open for 28% of the time, Pallas kernels for 0%

commit v1 on v0

--- a/solution.py
+++ b/solution.py
@@ -5,6 +5,11 @@
 
 SPAN = 128
 highest = lax.Precision.HIGHEST
+
+
+def one_after_other(array, first, second):
+    partial = lax.psum(array, first)
+    return lax.psum(partial, second)
 
 
 def prefix(shard, axis, combine, identity, reverse):
@@ -166,8 +171,8 @@
     )
     later_grad = prefix((through, start_grad), "seq", combine, identity, True)[1]
     x_grad, b_grad, c_grad, logit_grad, bias_grad, rate_grad = ssd_pullback((later_grad, y_grad))
-    bias_sum, rate_sum, skip_sum, gain_sum = lax.psum(
-        (bias_grad, rate_grad, skip_grad, gain_grad), ("dp", "seq")
+    bias_sum, rate_sum, skip_sum, gain_sum = one_after_other(
+        (bias_grad, rate_grad, skip_grad, gain_grad), "dp", "seq"
     )
     seq_rows = lax.psum_scatter(
         lax.dot_general(

time: 984 us -> 1060 us (1.077)
  blocking collectives: 88.7 us -> 159 us
    psum x1 -> x2, blocking collectives: 64.7 us -> 135 us  [the longest x1 122 us: one_after_other(): return lax.psum(partial, second)]
  transfers between devices with their start and end apart: 4 -> 4, of which waited for: 3 -> 3; matrix products, arithmetic and copies ran while one was open for 28% -> 26% of each run, Pallas kernels for 0% -> 0%
where the time goes in v1:
time: 1060 us; the launch traced here: 1040 us
  waiting for transfers between devices  325 us (31%)
  local copies, waits for them, and re-layouts  220 us (21%)
  other arithmetic  192 us (18%)
  blocking collectives  159 us (15%)
  matrix products  128 us (12%)
  between operations  15.1 us (1%)
    all_gather x2, waiting for transfers between devices, prefix(): everything = jax.tree.map(lambda part: lax.all_gather(part, axis), shard)  276 us
    psum x1, blocking collectives, one_after_other(): return lax.psum(partial, second)  122 us
    select_n x64, other arithmetic, hop(): return jax.tree.map(lambda a, b: jnp.where(reached, a, b), new, before)  113 us
    dynamic_update_slice x44, local copies, waits for them, and re-layouts, ssd_blocks(): lax.scan(block_step, state_in, (to_blocks(x_heads), to_blocks(b_float), t...  89 us
    reduce_scatter x1, waiting for transfers between devices, per_device(): lax.psum_scatter(lax.dot_general(normed, grad_rows, (((0,), (0,)), ((), (...  48.3 us
    dot_general x6, matrix products, block_step(): y_blk = jnp.einsum('ijh,jhp->ihp', mixing, x_blk, precision=highest)  48.3 us
    all_gather x1, blocking collectives, prefix(): everything = jax.tree.map(lambda part: lax.all_gather(part, axis), shard)  24 us
    mul x2, other arithmetic, block_step(): mixing = gram_mat[:, :, None] * decay_mat * step_blk[None, :, :]  22.6 us
  transfers between devices with their start and end apart: 4, of which 3 were waited for; matrix products, arithmetic and copies ran while one was open for 26% of the time, Pallas kernels for 0%

profile of v1, /device:TPU:1, one launch (start us, length us, event | category | flops | bytes accessed | tf_op | source)
XLA Modules:
  0.0 1044.1 jit_solution(6420701765702877311)
XLA Ops:
  17.8 3.7 copy.144
  21.5 4.1 convert_multiply_fusion
  25.6 3.6 copy.145
  29.2 4.5 fusion.162
  34.0 3.1 copy.147
  37.1 5.3 reshape.1003
  42.5 4.0 copy.148
  46.5 3.2 copy.152
  49.7 5.5 reshape.1008
  55.9 24.0 %all-gather.2 = f32[32,1,48]{2,1,0:T(1,128)S(1)} all-gather(f32[1,1,48]{2,1,0:T(1,128)S(1)} %bitcast.581), channel_id=1, replica_groups=mesh['dp'=4,'seq'=32] {'seq'}, dimensions={0}, use_global_device_ids=true | all-gather | bytes 6336 | tf_op jit(solution)/shard_map/all_gather | solution.py:17
  79.9 115.2 %all-gather.6.cloned.1.call-done = f32[1536,64,128]{2,1,0:T(8,128)} async-done(((f32[48,64,128]{2,1,0:T(8,128)}), f32[1536,64,128]{2,1,0:T(8,128)}) %all-gather.6.cloned.1.call-update) | async-done | bytes 50331664 | tf_op jit(solution)/shard_map/all_gather | solution.py:17
  195.1 58.0 %while.116 = (s32[]{:T(128)}, f32[48,64,128]{2,1,0:T(8,128)S(1)}, s32[]{:T(128)}, f32[32,48]{1,0:T(8,128)S(1)}, f32[32,48,64,128]{3,2,1,0:T(8,128)}, /*index=5*/s32[]{:T(128)}, s32[]{:T(128)}) while((s32[]{:T(128)}, f32[48,64,128]{2,1,0:T(8,128)S(1)}, s32[]{:T(128)}, f32[32,48]{1,0:T(8,128)S(1)}, f32[32,48,64,128]{3,2,1,0:T(8,128)}, ...), condition=%wide.region_6.7_spmd.clone, body=%wide.region_5.6_spmd.clone.sunk | while | flops 1572868 | bytes 4719273 | solution.py:30
  259.2 154.5 %while.115 = (s32[]{:T(128)}, f32[48,64,128]{2,1,0:T(8,128)S(1)}, f32[2,128,48,64]{1,3,2,0:T(8,128)}, pred[2,128,128,48]{2,1,3,0:T(32,128)(4,1)}, f32[2,128,128,...) while((s32[]{:T(128)}, f32[48,64,128]{2,1,0:T(8,128)S(1)}, ...), condition=%wide.region_10.11_spmd.clone, body=%wide.region_7.10_spmd.clone.sunk | while | flops 1848273152 | bytes 111490832 | solution.py:71
  262.9 11.3 %broadcast_multiply_fusion.4 = (f32[1,128,128,48]{3,2,1,0:T(8,128)}, f32[1,128,128,48]{3,2,1,0:T(8,128)}, f32[1,128,128,48]{3,2,1,0:T(8,128)}, f32[1,128,128,48]{3,2,1,0:T(8,128)}) fusion(f32[128,48]{1,0:T(8,128)S(1)} %get-tuple-element.2454, f32[128,48]{1,0:T(8,128)S(1)} %reduce_window_sum.92, pred[128,128]{1,0:T(8,128)(4,1)S(1)} %fusion.251, ...), kind=kLoop, calls=%fused_computation.99.clone.1 | loop fusion | flops 3932160 | bytes 12713984 | tf_op jit(solution)/shard_map/jvp()/while/body/eval_jaxpr/mul | solution.py:44
  274.2 6.9 copy.272
  281.1 6.8 copy.273
  287.9 6.3 constant_dynamic-update-slice_fusion.23
  294.2 6.9 copy.269
  301.1 6.8 copy.270
  307.9 6.4 constant_dynamic-update-slice_fusion.21
  317.1 7.6 bitcast_dynamic-update-slice_fusion.13
  324.7 2.9 multiply_dynamic-update-slice_fusion.2
  339.9 11.3 %broadcast_multiply_fusion.4 = (f32[1,128,128,48]{3,2,1,0:T(8,128)}, f32[1,128,128,48]{3,2,1,0:T(8,128)}, f32[1,128,128,48]{3,2,1,0:T(8,128)}, f32[1,128,128,48]{3,2,1,0:T(8,128)}) fusion(f32[128,48]{1,0:T(8,128)S(1)} %get-tuple-element.2454, f32[128,48]{1,0:T(8,128)S(1)} %reduce_window_sum.92, pred[128,128]{1,0:T(8,128)(4,1)S(1)} %fusion.251, ...), kind=kLoop, calls=%fused_computation.99.clone.1 | loop fusion | flops 3932160 | bytes 12713984 | tf_op jit(solution)/shard_map/jvp()/while/body/eval_jaxpr/mul | solution.py:44
  351.2 6.9 copy.272
  358.1 6.8 copy.273
  365.0 6.3 constant_dynamic-update-slice_fusion.23
  371.2 6.9 copy.269
  378.1 6.8 copy.270
  384.9 6.4 constant_dynamic-update-slice_fusion.21
  391.6 2.6 bitcast_dynamic-update-slice_fusion.11
  394.2 7.6 bitcast_dynamic-update-slice_fusion.13
  401.8 2.9 multiply_dynamic-update-slice_fusion.2
  413.7 7.7 multiply_reduce_fusion.2
  421.4 3.9 multiply_convert_fusion
  425.3 7.8 fusion.146
  436.0 3.6 copy.153
  439.6 6.5 copy.180
  446.1 6.4 reshape.1022
  452.5 10.8 %multiply_reduce_fusion = (f32[3072]{0:T(1024)}, f32[256]{0:T(256)S(1)}, f32[256,3072]{1,0:T(8,128)S(1)}) fusion(f32[256]{0:T(256)S(1)} %bitcast_rsqrt_fusion, bf16[1,256,3072]{2,1,0:T(8,128)(2,1)} %param.21, f32[256,3072]{1,0:T(8,128)} %reshape.1022, f32[3072]{0:T(1024)S(1)} %mul.708, bf16[1,256,3072]{2,1,0:T(8,128)(2,1)S(1)} %copy-done.8, ...), kind=kOutput, calls=%fused_computation.207 | convolution fusion | flops 2427712256 | bytes 19699712 | tf_op jit(solution)/shard_map/dot_general | solution.py:165
  463.3 3.9 fusion.142
  471.0 4.1 copy.154
  475.1 4.6 fusion.160
  480.5 6.1 reshape.1023
  486.6 7.1 copy.158
  494.4 10.0 fusion.143
  504.3 48.3 %reduce-scatter.2.cloned.1.call-done = f32[96,1536]{1,0:T(8,128)} async-done(((f32[3072,1536]{1,0:T(8,128)}), f32[96,1536]{1,0:T(8,128)}) %reduce-scatter.2.cloned.1.call-update) | async-done | bytes 589840 | tf_op jit(solution)/shard_map/reduce_scatter | solution.py:177
  552.7 161.2 %all-gather.8.cloned.1.call-done = f32[1536,64,128]{2,1,0:T(8,128)} async-done(((f32[48,64,128]{2,1,0:T(8,128)}), f32[1536,64,128]{2,1,0:T(8,128)}) %all-gather.8.cloned.1.call-update) | async-done | bytes 50331664 | tf_op jit(solution)/shard_map/all_gather | solution.py:17
  713.8 79.9 %while.117 = (s32[]{:T(128)}, f32[48,64,128]{2,1,0:T(8,128)S(1)}, s32[]{:T(128)}, f32[32,48]{1,0:T(8,128)}, f32[32,48,64,128]{3,2,1,0:T(8,128)}, /*index=5*/s32[]{:T(128)}, s32[]{:T(128)}, s32[]{:T(128)}, s32[]{:T(128)}) while((s32[]{:T(128)}, f32[48,64,128]{2,1,0:T(8,128)S(1)}, s32[]{:T(128)}, f32[32,48]{1,0:T(8,128)}, ...), condition=%wide.region_14.15_spmd.clone, body=%wide.region_13.14_spmd.clone.sunk | while | flops 1572872 | bytes 4719335 | solution.py:30
  797.9 83.0 %while.114 = (s32[]{:T(128)}, f32[48,64,128]{2,1,0:T(8,128)S(1)}, f32[2,128,48,64]{1,3,2,0:T(8,128)}, bf16[2,128,128]{2,1,0:T(8,128)(2,1)}, bf16[2,128,128]{2,1,...) while((s32[]{:T(128)}, f32[48,64,128]{2,1,0:T(8,128)S(1)}, ...), condition=%wide.region_25.26_spmd, body=%wide.region_15.25_spmd.sunk | while | flops 3688450048 | bytes 77251128 | solution.py:71
  798.9 11.1 %fusion.235 = (f32[128,48]{0,1:T(8,128)S(1)}, f32[128,48]{0,1:T(8,128)S(1)}, f32[128,128]{1,0:T(8,128)S(1)}, f32[128,48]{0,1:T(8,128)S(1)}) fusion(f32[2,128,128,48]{2,1,3,0:T(8,128)} %get-tuple-element.2732, s32[]{:T(128)S(6)} %sub.274, f32[128,48]{0,1:T(8,128)S(1)} %dynamic-slice_bitcast_fusion.18, ...), kind=kOutput, calls=%fused_computation.91.clone.1 | convolution fusion | flops 612595712 | bytes 13600256 | tf_op jit(solution)/shard_map/transpose(jvp())/while/body/eval_jaxpr/ijh,jhp->ihp/dot_general | solution.py:45
  812.0 4.0 fusion.233
  821.9 4.7 fusion.237
  827.4 4.0 fusion.234
  831.8 5.5 bitcast_dynamic-update-slice_fusion.10
  840.2 11.1 %fusion.235 = (f32[128,48]{0,1:T(8,128)S(1)}, f32[128,48]{0,1:T(8,128)S(1)}, f32[128,128]{1,0:T(8,128)S(1)}, f32[128,48]{0,1:T(8,128)S(1)}) fusion(f32[2,128,128,48]{2,1,3,0:T(8,128)} %get-tuple-element.2732, s32[]{:T(128)S(6)} %sub.274, f32[128,48]{0,1:T(8,128)S(1)} %dynamic-slice_bitcast_fusion.18, ...), kind=kOutput, calls=%fused_computation.91.clone.1 | convolution fusion | flops 612595712 | bytes 13600256 | tf_op jit(solution)/shard_map/transpose(jvp())/while/body/eval_jaxpr/ijh,jhp->ihp/dot_general | solution.py:45
  853.3 4.0 fusion.233
  863.2 4.7 fusion.237
  868.8 4.0 fusion.234
  873.2 5.4 bitcast_dynamic-update-slice_fusion.10
  883.0 6.1 copy.183
  889.1 5.8 reshape.1024
  895.7 13.0 %all-reduce.3 = (f32[48]{0:T(128)S(1)}, f32[48]{0:T(128)S(1)}, f32[48]{0:T(128)S(1)}, f32[3072]{0:T(1024)S(1)}) all-reduce(f32[48]{0:T(128)S(1)} %get-tuple-element.1778, f32[48]{0:T(128)S(1)} %neg.49, f32[48]{0:T(128)S(1)} %copy-done.36, f32[3072]{0:T(1024)S(1)} %copy-done.32), channel_id=1, replica_groups=mesh['dp'=4,'seq'=32] {'dp'}, use_global_device_ids=true, to_apply=%region_27.28 | all-reduce | flops 3216 | bytes 25728 | tf_op jit(solution)/shard_map/psum | solution.py:11
  908.7 122.1 %all-reduce.2 = (f32[48]{0:T(128)}, f32[48]{0:T(128)}, f32[48]{0:T(128)}, f32[3072]{0:T(1024)}) all-reduce(f32[48]{0:T(128)S(1)} %get-tuple-element.1927, f32[48]{0:T(128)S(1)} %get-tuple-element.1928, f32[48]{0:T(128)S(1)} %get-tuple-element.1929, f32[3072]{0:T(1024)S(1)} %get-tuple-element.1930), channel_id=1, replica_groups=mesh['dp'=4,'seq'=32] {'seq'}, use_global_device_ids=true, to_apply=%region_28.29 | all-reduce | flops 3216 | bytes 25728 | tf_op jit(solution)/shard_map/psum | solution.py:12
  1030.8 4.6 fusion.145
  (450 shorter events, 219.7 us)
Async XLA Ops:
  7.2 418.2 %copy-start = (bf16[1,256,1536]{2,1,0:T(8,128)(2,1)S(1)}, bf16[1,256,1536]{2,1,0:T(8,128)(2,1)}, u32[]{:S(2)}) copy-start(bf16[1,256,1536]{2,1,0:T(8,128)(2,1)} %param.31) | copy-start | bytes 2359300
  7.2 187.9 %all-gather.6.cloned.1.call-start = ((), (), s32[]{:S(2)}) async-start(), calls=%async_computation.3 | async-start | bytes 51904512 | tf_op jit(solution)/shard_map/all_gather | solution.py:17
  12.5 67.4 %copy-start.33 = (f32[48]{0:T(128)}, f32[48]{0:T(128)S(1)}, u32[]{:S(2)}) copy-start(f32[48]{0:T(128)S(1)} %neg.43) | copy-start | bytes 580
  17.8 3.7 copy-start.7
  25.6 3.6 copy-start.16
  29.2 4.6 copy-start.14
  33.8 518.9 %reduce-scatter.2.cloned.1.call-start = ((), (), s32[]{:S(2)}) async-start(), calls=%async_computation.1 | async-start | bytes 19464192 | tf_op jit(solution)/shard_map/reduce_scatter | solution.py:177
  33.9 45.9 %copy-start.12 = (f32[1,256,48]{2,1,0:T(8,128)}, f32[1,256,48]{2,1,0:T(8,128)S(1)}, u32[]{:S(2)}) copy-start(f32[1,256,48]{2,1,0:T(8,128)S(1)} %copy.179) | copy-start | bytes 147460
  42.5 4.0 copy-start.17
  49.7 5.5 copy-start.26
  49.7 30.2 %copy-start.29 = (f32[48]{0:T(128)S(1)}, f32[48]{0:T(128)}, u32[]{:S(2)}) copy-start(f32[48]{0:T(128)} %param.25) | copy-start | bytes 580
  253.1 4.1 copy-start.28
  314.5 2.6 copy-start.2
  328.3 2.5 copy-start.3
  330.7 3.5 copy-start.21
  330.7 3.5 copy-start.40
  330.7 3.6 copy-start.31
  330.7 3.6 copy-start.37
  330.8 4.9 copy-start.43
  334.3 2.2 copy-start.22
  334.3 2.1 copy-start.41
  334.4 2.1 copy-start.38
  335.7 0.7 copy-start.44
  391.6 2.6 copy-start.2
  405.3 2.5 copy-start.3
  407.8 3.5 copy-start.21
  407.8 3.5 copy-start.40
  407.8 3.5 copy-start.31
  407.8 3.6 copy-start.37
  407.8 4.9 copy-start.43
  411.3 2.2 copy-start.22
  411.3 2.1 copy-start.41
  411.4 2.1 copy-start.38
  413.7 7.7 copy-start.20
  433.1 0.8 copy-start.19
  433.2 280.7 %all-gather.8.cloned.1.call-start = ((), (), s32[]{:S(2)}) async-start(), calls=%async_computation.4 | async-start | bytes 51904512 | tf_op jit(solution)/shard_map/all_gather | solution.py:17
  446.1 6.4 copy-start.8
  446.1 6.4 copy-start.27
  452.5 10.8 %copy-start.10 = (f32[256,3072]{1,0:T(8,128)S(1)}, f32[256,3072]{1,0:T(8,128)}, u32[]{:S(2)}) copy-start(f32[256,3072]{1,0:T(8,128)} %reshape.1022) | copy-start | bytes 9437188
  452.5 10.8 %copy-start.11 = (bf16[1,256,3072]{2,1,0:T(8,128)(2,1)S(1)}, bf16[1,256,3072]{2,1,0:T(8,128)(2,1)}, u32[]{:S(2)}) copy-start(bf16[1,256,3072]{2,1,0:T(8,128)(2,1)} %param.21) | copy-start | bytes 4718596
  463.3 5.6 copy-start.9
  467.2 1.6 copy-start.6
  471.0 4.1 copy-start.18
  479.8 555.6 %all-reduce.6.cloned.1.call-start = ((), (), s32[]{:S(2)}) async-start(), calls=%async_computation.2 | async-start | bytes 1179648 | tf_op jit(solution)/shard_map/psum | solution.py:185
  793.7 4.2 copy-start.23
  793.7 4.1 copy-start.39
  793.7 4.1 copy-start.42
  793.7 4.1 copy-start.45
  797.9 84.8 %copy-start.13 = (f32[1,256,48]{2,1,0:T(8,128)S(1)}, f32[1,256,48]{2,1,0:T(8,128)}, u32[]{:S(2)}) copy-start(f32[1,256,48]{2,1,0:T(8,128)} %copy-done.12) | copy-start | bytes 147460
  797.9 84.8 %copy-start.30 = (f32[48]{0:T(128)S(1)}, f32[48]{0:T(128)}, u32[]{:S(2)}) copy-start(f32[48]{0:T(128)} %param.25) | copy-start | bytes 580
  797.9 84.8 %copy-start.34 = (f32[48]{0:T(128)S(1)}, f32[48]{0:T(128)}, u32[]{:S(2)}) copy-start(f32[48]{0:T(128)} %copy-done.33) | copy-start | bytes 580
  798.9 11.2 %copy-start.5 = (f32[2,48,64,128]{3,2,1,0:T(8,128)S(1)}, f32[2,48,64,128]{3,2,1,0:T(8,128)}, u32[]{:S(2)}) copy-start(f32[2,48,64,128]{3,2,1,0:T(8,128)} %get-tuple-element.2719) | copy-start | bytes 9437188 | tf_op jit(solution)/shard_map/transpose(jvp())/while
  821.9 9.6 copy-start.24
  821.9 9.9 copy-start.1
  821.9 9.9 copy-start.4
  831.8 5.5 copy-start.25
  840.2 11.2 %copy-start.5 = (f32[2,48,64,128]{3,2,1,0:T(8,128)S(1)}, f32[2,48,64,128]{3,2,1,0:T(8,128)}, u32[]{:S(2)}) copy-start(f32[2,48,64,128]{3,2,1,0:T(8,128)} %get-tuple-element.2719) | copy-start | bytes 9437188 | tf_op jit(solution)/shard_map/transpose(jvp())/while
  863.2 9.6 copy-start.24
  863.2 9.9 copy-start.1
  863.2 9.9 copy-start.4
  873.1 5.4 copy-start.25
  889.1 5.9 copy-start.15
  889.1 6.6 copy-start.32
  889.1 6.6 copy-start.36
  (2 other events, 1.4 us)
Sparse Core Ops, SparseCore 0:
  33.9 161.1 all-gather.5
  433.3 119.3 reduce-scatter.1
  555.8 158.0 all-gather.7
  716.2 40.1 all-reduce.5
